TPU v7x, 128 devices: a whole 4x4x4 slice. The times are simulated.
128 devices in a mesh: row: 8 (over z_lo, x), col: 16 (over y, z_hi, core).
Axes of the slice: x: 4, y: 4, z: 4 (z_hi: 2, z_lo: 2; z = z_hi * 2 + z_lo), core: 2. Of those that a mesh axis runs over, the one named last changes fastest.
Arguments:
- tokens_map: bfloat16 [512, 1024, 384], P('row', 'col'), may hold values from -6 to 6
- gain_attn: float32 [384], replicated, may hold values from 0.1 to 1.9
- w_qkv: bfloat16 [384, 1152], replicated, may hold values from -1 to 1
- w_proj: bfloat16 [384, 384], replicated, may hold values from -0.3125 to 0.3125
- rel_bias: float32 [12, 15, 15], replicated, may hold values from -4 to 4
- gain_mlp: float32 [384], replicated, may hold values from 0.1 to 1.9
- w_up: bfloat16 [384, 1536], replicated, may hold values from -0.3125 to 0.3125
- w_down: bfloat16 [1536, 384], replicated, may hold values from -0.15625 to 0.15625
Outputs:
- block_out: bfloat16 [512, 1024, 384], P('row', 'col')
All inputs are finite; a program needn't handle non-finite values.
Results may differ from a plain program's by a relative error of at most 0.0062.
Values may be sent and summed in bfloat16 or wider, within the bound.
A program may use at most 192 MiB of HBM per device.

v0:
```python
import math

import jax
import jax.numpy as jnp
from jax import lax
from jax.experimental import pallas as pl
from jax.experimental.pallas import tpu as pltpu
from jax.sharding import PartitionSpec as P

MESH = pl.DeviceIdType.MESH
f32, bf16 = jnp.float32, jnp.bfloat16

D = 384
HEADS = 12
HEAD_DIM = 32
MLP_DIM = 1536
GRID = 8
MEMBERS = GRID * GRID
EPSILON = 1e-5
LOG2E = math.log2(math.e)

CHUNK = 16
TILE = 16
CHUNKS = 4
ATTN_TILES = 4
MLP_TILES = 2


def norm(values, gain):
    average = jnp.mean(values, -1, keepdims=True)
    centered = values - average
    variance = jnp.mean(centered * centered, -1, keepdims=True)
    return (centered * lax.rsqrt(variance + EPSILON) * gain).astype(bf16)


def fill_swap(swap):
    r = lax.broadcasted_iota(jnp.int32, (256, 256), 0)
    c = lax.broadcasted_iota(jnp.int32, (256, 256), 1)
    swap[...] = ((r // 16 == c % 16) & (r % 16 == c // 16)).astype(bf16)


def fill_ones(ones):
    r = lax.broadcasted_iota(jnp.int32, (256, 128), 0)
    c = lax.broadcasted_iota(jnp.int32, (256, 128), 1)
    ones[...] = (r // MEMBERS == c // HEAD_DIM).astype(bf16)


def fill_bias(rel, strip, bias):
    s = lax.broadcasted_iota(jnp.int32, (15, 1024), 0)
    lane = lax.broadcasted_iota(jnp.int32, (15, 1024), 1)
    g2i, q, g2j = lane // 128, (lane % 128) // 8, lane % 8
    hits = ((s == g2i - g2j + 7) & (q < 15)).astype(f32)
    rows = s == 14 - q
    for h in range(HEADS):
        spread = jnp.dot(rel[h], hits, preferred_element_type=f32, precision=lax.Precision.HIGHEST)
        line = jnp.sum(jnp.where(rows, spread, 0.0), 0, keepdims=True) * LOG2E
        for g in range(GRID):
            strip[h, g:g + 1, :] = line[:, g * 128:(g + 1) * 128]
    for h in range(HEADS):
        u = strip[h]
        for g1 in range(GRID):
            at = (GRID - 1 - g1) * GRID
            lanes = slice((h % 4) * MEMBERS, (h % 4 + 1) * MEMBERS)
            bias[h // 4, g1 * GRID:(g1 + 1) * GRID, lanes] = u[:, at:at + MEMBERS]


def turn(swap, rows):
    parts = [
        jnp.dot(swap, rows[at:at + 256], preferred_element_type=f32).astype(bf16)
        for at in range(0, rows.shape[0], 256)
    ]
    return parts[0] if len(parts) == 1 else jnp.concatenate(parts, 0)


def project(step, tokens, gain, w_qkv, swap, qkv):
    first = step * ATTN_TILES * TILE
    x = tokens[pl.ds(first, ATTN_TILES * TILE)].reshape(ATTN_TILES * 256, D).astype(f32)
    turned = turn(swap[...], norm(x, gain))
    packed = jnp.dot(turned, w_qkv[...], preferred_element_type=f32).astype(bf16)
    for part in range(3):
        for t in range(ATTN_TILES):
            block = packed[t * 256:(t + 1) * 256, part * D:(part + 1) * D]
            qkv[part, :, pl.ds(first + t * TILE, TILE), :] = block.reshape(CHUNK, TILE, D)


def attend(b, qkv, bias, ones, mix):
    lane = lax.broadcasted_iota(jnp.int32, (1, 128), 1)
    low = lane < MEMBERS
    masks = [(lane // HEAD_DIM == h).astype(bf16) for h in range(4)]
    for hb in range(3):
        cols = slice(hb * 128, (hb + 1) * 128)
        q = qkv[0, b, :, cols]
        k = qkv[1, b, :, cols]
        v = qkv[2, b, :, cols]
        keys = jnp.concatenate([k * m for m in masks], 0)
        values = jnp.concatenate([v * m for m in masks], 0)
        scores = lax.dot_general(q, keys, (((1,), (1,)), ((), ())), preferred_element_type=f32)
        scores = scores * (HEAD_DIM ** -0.5 * LOG2E) + bias[hb]
        weights = []
        for pair in range(2):
            s = scores[:, pair * 128:(pair + 1) * 128]
            peak0 = jnp.max(jnp.where(low, s, -jnp.inf), -1, keepdims=True)
            peak1 = jnp.max(jnp.where(low, -jnp.inf, s), -1, keepdims=True)
            weights.append(jnp.exp2(s - jnp.where(low, peak0, peak1)).astype(bf16))
        sums = jnp.dot(
            jnp.concatenate(weights, 1),
            jnp.concatenate([values, ones[...]], 1),
            preferred_element_type=f32,
        )
        mixture = (sums[:, :128] / sums[:, 128:]).astype(bf16)
        mix[:, pl.ds(b, 1), :, cols] = mixture.reshape(MEMBERS // TILE, 1, TILE, 128)


def finish(step, tokens, mix, swap, w_proj, gain, w_up, w_down, done):
    rows = MLP_TILES * 256
    first = step * MLP_TILES * TILE
    x = tokens[pl.ds(first, MLP_TILES * TILE)].reshape(rows, D).astype(f32)
    mixture = turn(swap[...], mix[pl.ds(step * MLP_TILES, MLP_TILES)].reshape(rows, D))
    attended = (x + jnp.dot(mixture, w_proj[...], preferred_element_type=f32)).astype(bf16)
    normed = norm(attended.astype(f32), gain)
    hidden = []
    for c in range(0, MLP_DIM, 512):
        u = jnp.dot(normed, w_up[:, c:c + 512], preferred_element_type=f32)
        hidden.append((u * (0.5 * lax.erf(u * (2 ** -0.5)) + 0.5)).astype(bf16))
    total = attended.astype(f32) + jnp.dot(
        jnp.concatenate(hidden, 1), w_down[...], preferred_element_type=f32
    )
    done[pl.ds(first, MLP_TILES * TILE)] = total.astype(bf16).reshape(MLP_TILES * TILE, CHUNK, D)


def kernel(
    x_ref, gain_attn, wq_ref, wp_ref, rel, gain_mlp, wu_ref, wd_ref,
    out_ref,
    tokens, done, w_qkv, w_proj, w_up, w_down, qkv, mix, bias, strip, swap, ones,
    weight_sem, in_sem, sent_sem, back_sem, out_sem,
):
    g1 = lax.axis_index("row")
    col = lax.axis_index("col")
    g2, core = col // 2, col % 2
    me = g1 * GRID + g2

    def partner(t):
        p1, p2 = lax.rem(g1 + t // GRID, GRID), lax.rem(g2 + lax.rem(t, GRID), GRID)
        return p1 * GRID + p2, (p1, p2 * 2 + core)

    barrier = pltpu.get_barrier_semaphore()

    @pl.loop(1, MEMBERS)
    def _(t):
        pl.semaphore_signal(barrier, inc=1, device_id=partner(t)[1], device_id_type=MESH)

    weights = [
        pltpu.make_async_copy(src, dst, weight_sem.at[i])
        for i, (src, dst) in enumerate(
            ((wq_ref, w_qkv), (wp_ref, w_proj), (wu_ref, w_up), (wd_ref, w_down))
        )
    ]
    for c in range(CHUNKS):
        pltpu.make_async_copy(
            x_ref.at[me, pl.ds(c * CHUNK, CHUNK)], tokens.at[c, me], in_sem.at[c]
        ).start()
    for copy in weights:
        copy.start()
    pl.semaphore_wait(barrier, MEMBERS - 1)

    for c in range(CHUNKS):

        @pl.loop(1, MEMBERS)
        def _(t):
            peer, device = partner(t)
            pltpu.make_async_remote_copy(
                src_ref=x_ref.at[peer, pl.ds(c * CHUNK, CHUNK)],
                dst_ref=tokens.at[c, me],
                send_sem=sent_sem.at[0],
                recv_sem=in_sem.at[c],
                device_id=device,
                device_id_type=MESH,
            ).start()

    fill_swap(swap)
    fill_ones(ones)
    fill_bias(rel, strip, bias)
    for copy in weights:
        copy.wait()

    @pl.loop(0, CHUNKS)
    def _(c):
        here = tokens.at[c]
        pltpu.make_async_copy(here, here, in_sem.at[c]).wait()

        @pl.loop(0, MEMBERS // TILE // ATTN_TILES)
        def _(step):
            project(step, here, gain_attn[...][None], w_qkv, swap, qkv)

        @pl.loop(0, CHUNK, unroll=True)
        def _(b):
            attend(b, qkv, bias, ones, mix)

        @pl.loop(0, MEMBERS // TILE // MLP_TILES)
        def _(step):
            finish(
                step, here, mix, swap, w_proj, gain_mlp[...][None], w_up, w_down, done.at[c]
            )
            rows = MLP_TILES * TILE

            @pl.loop(step * rows, (step + 1) * rows)
            def _(m):
                @pl.when(m != me)
                def _():
                    pltpu.make_async_remote_copy(
                        src_ref=done.at[c, m],
                        dst_ref=out_ref.at[me, pl.ds(c * CHUNK, CHUNK)],
                        send_sem=back_sem.at[0],
                        recv_sem=out_sem.at[0],
                        device_id=(m // GRID, (m % GRID) * 2 + core),
                        device_id_type=MESH,
                    ).start()

                @pl.when(m == me)
                def _():
                    pltpu.make_async_copy(
                        done.at[c, m], out_ref.at[me, pl.ds(c * CHUNK, CHUNK)], out_sem.at[0]
                    ).start()

    pltpu.make_async_copy(out_ref, out_ref, out_sem.at[0]).wait()
    others = x_ref.at[pl.ds(0, MEMBERS - 1)]
    pltpu.make_async_copy(others, others, sent_sem.at[0]).wait()
    pltpu.make_async_copy(others, others, back_sem.at[0]).wait()


def on_device(tokens_map, gain_attn, w_qkv, w_proj, rel_bias, gain_mlp, w_up, w_down):
    hbm = pl.BlockSpec(memory_space=pl.ANY)
    vmem = pl.BlockSpec(memory_space=pltpu.VMEM)
    return pl.pallas_call(
        kernel,
        name="grid_block",
        out_shape=jax.ShapeDtypeStruct(tokens_map.shape, bf16),
        in_specs=[hbm, vmem, hbm, hbm, vmem, vmem, hbm, hbm],
        out_specs=hbm,
        scratch_shapes=[
            pltpu.VMEM((CHUNKS, MEMBERS, CHUNK, D), bf16),
            pltpu.VMEM((CHUNKS, MEMBERS, CHUNK, D), bf16),
            pltpu.VMEM((D, 3 * D), bf16),
            pltpu.VMEM((D, D), bf16),
            pltpu.VMEM((D, MLP_DIM), bf16),
            pltpu.VMEM((MLP_DIM, D), bf16),
            pltpu.VMEM((3, CHUNK, MEMBERS, D), bf16),
            pltpu.VMEM((MEMBERS // TILE, CHUNK, TILE, D), bf16),
            pltpu.VMEM((3, MEMBERS, 4 * MEMBERS), f32),
            pltpu.VMEM((HEADS, GRID, 128), f32),
            pltpu.VMEM((256, 256), bf16),
            pltpu.VMEM((256, 128), bf16),
            pltpu.SemaphoreType.DMA((4,)),
            pltpu.SemaphoreType.DMA((CHUNKS,)),
            pltpu.SemaphoreType.DMA((1,)),
            pltpu.SemaphoreType.DMA((1,)),
            pltpu.SemaphoreType.DMA((1,)),
        ],
        compiler_params=pltpu.CompilerParams(
            collective_id=0, has_side_effects=True, vmem_limit_bytes=56 * 2**20
        ),
    )(tokens_map, gain_attn, w_qkv, w_proj, rel_bias, gain_mlp, w_up, w_down)


def solution(mesh):
    placed = (P("row", "col", None), P(), P(), P(), P(), P(), P(), P())
    return jax.shard_map(
        on_device, mesh=mesh, in_specs=placed, out_specs=P("row", "col", None), check_vma=False
    )
```

profile of v0, /device:TPU:62, one launch (start us, length us, event | category | flops | bytes accessed | tf_op | source)
XLA Modules:
  0.0 99.7 jit_solution(856367618098932541)
XLA Ops:
  0.0 95.8 %grid_block.1 = bf16[64,64,384]{2,1,0:T(8,128)(2,1)} custom-call(bf16[64,64,384]{2,1,0:T(8,128)(2,1)} %x_ref.1, f32[384]{0:T(512)} %gain_attn.1, bf16[384,1152]{1,0:T(8,128)(2,1)} %wq_ref.1, bf16[384,384]{1,0:T(8,128)(2,1)} %wp_ref.1, f32[12,15,15]{2,1,0:T(8,128)} %rel.1, f32[384]{0:T(512)} %gain_mlp.1, bf16[384,1536]{1,0:T(8,128)(2,1)} %wu_ref.1, ...), custom_call_target="tpu_custom_call" | custom-call | tf_op jit(solution)/shard_map/grid_block/pallas_call | solution.py:234
  95.8 3.9 %copy.10 = bf16[64,64,384]{2,1,0:T(8,128)(2,1)} copy(bf16[64,64,384]{2,1,0:T(8,128)(2,1)} %grid_block.1) | data formatting | bytes 6291456
where the time goes:
time: 99.9 us; the launch traced here: 99.7 us
  Pallas kernels  95.8 us (96%)
  local copies, waits for them, and re-layouts  3.88 us (4%)
    pallas_call x1, Pallas kernels, on_device(): pl.pallas_call(kernel, name='grid_block', out_shape=jax.ShapeDtypeStruct(...  95.8 us
    unnamed x1, local copies, waits for them, and re-layouts  3.88 us

commit v1 on v0

--- a/solution.py
+++ b/solution.py
@@ -23,7 +23,7 @@
 TILE = 16
 CHUNKS = 4
 ATTN_TILES = 4
-MLP_TILES = 2
+MLP_TILES = 4
 
 
 def norm(values, gain):
@@ -201,26 +201,22 @@
             finish(
                 step, here, mix, swap, w_proj, gain_mlp[...][None], w_up, w_down, done.at[c]
             )
-            rows = MLP_TILES * TILE
-
-            @pl.loop(step * rows, (step + 1) * rows)
-            def _(m):
-                @pl.when(m != me)
-                def _():
-                    pltpu.make_async_remote_copy(
-                        src_ref=done.at[c, m],
-                        dst_ref=out_ref.at[me, pl.ds(c * CHUNK, CHUNK)],
-                        send_sem=back_sem.at[0],
-                        recv_sem=out_sem.at[0],
-                        device_id=(m // GRID, (m % GRID) * 2 + core),
-                        device_id_type=MESH,
-                    ).start()
-
-                @pl.when(m == me)
-                def _():
-                    pltpu.make_async_copy(
-                        done.at[c, m], out_ref.at[me, pl.ds(c * CHUNK, CHUNK)], out_sem.at[0]
-                    ).start()
+
+        @pl.loop(1, MEMBERS)
+        def _(t):
+            m, device = partner(t)
+            pltpu.make_async_remote_copy(
+                src_ref=done.at[c, m],
+                dst_ref=out_ref.at[me, pl.ds(c * CHUNK, CHUNK)],
+                send_sem=back_sem.at[0],
+                recv_sem=out_sem.at[0],
+                device_id=device,
+                device_id_type=MESH,
+            ).start()
+
+        pltpu.make_async_copy(
+            done.at[c, me], out_ref.at[me, pl.ds(c * CHUNK, CHUNK)], out_sem.at[0]
+        ).start()
 
     pltpu.make_async_copy(out_ref, out_ref, out_sem.at[0]).wait()
     others = x_ref.at[pl.ds(0, MEMBERS - 1)]

time: 99.9 us -> 85.3 us (0.85)
  the two profiles are of different devices: /device:TPU:62 before, /device:TPU:1 now
where the time goes in v1:
time: 85.3 us; the launch traced here: 84.4 us
  Pallas kernels  80.5 us (94%)
  local copies, waits for them, and re-layouts  3.88 us (5%)
    pallas_call x1, Pallas kernels, on_device(): pl.pallas_call(kernel, name='grid_block', out_shape=jax.ShapeDtypeStruct(...  80.5 us
    unnamed x1, local copies, waits for them, and re-layouts  3.88 us

profile of v1, /device:TPU:1, one launch (start us, length us, event | category | flops | bytes accessed | tf_op | source)
XLA Modules:
  0.0 84.4 jit_solution(5230540905215725948)
XLA Ops:
  0.0 80.5 %grid_block.1 = bf16[64,64,384]{2,1,0:T(8,128)(2,1)} custom-call(bf16[64,64,384]{2,1,0:T(8,128)(2,1)} %x_ref.1, f32[384]{0:T(512)} %gain_attn.1, bf16[384,1152]{1,0:T(8,128)(2,1)} %wq_ref.1, bf16[384,384]{1,0:T(8,128)(2,1)} %wp_ref.1, f32[12,15,15]{2,1,0:T(8,128)} %rel.1, f32[384]{0:T(512)} %gain_mlp.1, bf16[384,1536]{1,0:T(8,128)(2,1)} %wu_ref.1, ...), custom_call_target="tpu_custom_call" | custom-call | tf_op jit(solution)/shard_map/grid_block/pallas_call | solution.py:230
  80.5 3.9 %copy.10 = bf16[64,64,384]{2,1,0:T(8,128)(2,1)} copy(bf16[64,64,384]{2,1,0:T(8,128)(2,1)} %grid_block.1) | data formatting | bytes 6291456

commit v2 on v1

--- a/solution.py
+++ b/solution.py
@@ -22,8 +22,24 @@
 CHUNK = 16
 TILE = 16
 CHUNKS = 4
-ATTN_TILES = 4
-MLP_TILES = 4
+TILES = MEMBERS // TILE
+
+
+def displacements():
+    def hops(d):
+        return sum(min(v, 4 - v) for v in d)
+
+    order = []
+    for d in sorted(((x, y, z) for x in range(4) for y in range(4) for z in range(4)), key=hops):
+        group = []
+        for base in (d, tuple((4 - v) % 4 for v in d)):
+            group += [base[k:] + base[:k] for k in range(3)]
+        if d != (0, 0, 0) and d not in sum(order, []):
+            order.append(list(dict.fromkeys(group)))
+    return sum(reversed(order), [])
+
+
+ORDER = displacements()
 
 
 def norm(values, gain):
@@ -72,13 +88,12 @@
     return parts[0] if len(parts) == 1 else jnp.concatenate(parts, 0)
 
 
-def project(step, tokens, gain, w_qkv, swap, qkv):
-    first = step * ATTN_TILES * TILE
-    x = tokens[pl.ds(first, ATTN_TILES * TILE)].reshape(ATTN_TILES * 256, D).astype(f32)
+def project(first, tiles, tokens, gain, w_qkv, swap, qkv):
+    x = tokens[pl.ds(first, tiles * TILE)].reshape(tiles * 256, D).astype(f32)
     turned = turn(swap[...], norm(x, gain))
     packed = jnp.dot(turned, w_qkv[...], preferred_element_type=f32).astype(bf16)
     for part in range(3):
-        for t in range(ATTN_TILES):
+        for t in range(tiles):
             block = packed[t * 256:(t + 1) * 256, part * D:(part + 1) * D]
             qkv[part, :, pl.ds(first + t * TILE, TILE), :] = block.reshape(CHUNK, TILE, D)
 
@@ -111,11 +126,10 @@
         mix[:, pl.ds(b, 1), :, cols] = mixture.reshape(MEMBERS // TILE, 1, TILE, 128)
 
 
-def finish(step, tokens, mix, swap, w_proj, gain, w_up, w_down, done):
-    rows = MLP_TILES * 256
-    first = step * MLP_TILES * TILE
-    x = tokens[pl.ds(first, MLP_TILES * TILE)].reshape(rows, D).astype(f32)
-    mixture = turn(swap[...], mix[pl.ds(step * MLP_TILES, MLP_TILES)].reshape(rows, D))
+def finish(first, tiles, tokens, mix, swap, w_proj, gain, w_up, w_down, done):
+    rows = tiles * 256
+    x = tokens[pl.ds(first * TILE, tiles * TILE)].reshape(rows, D).astype(f32)
+    mixture = turn(swap[...], mix[pl.ds(first, tiles)].reshape(rows, D))
     attended = (x + jnp.dot(mixture, w_proj[...], preferred_element_type=f32)).astype(bf16)
     normed = norm(attended.astype(f32), gain)
     hidden = []
@@ -125,49 +139,52 @@
     total = attended.astype(f32) + jnp.dot(
         jnp.concatenate(hidden, 1), w_down[...], preferred_element_type=f32
     )
-    done[pl.ds(first, MLP_TILES * TILE)] = total.astype(bf16).reshape(MLP_TILES * TILE, CHUNK, D)
+    done[pl.ds(first * TILE, tiles * TILE)] = total.astype(bf16).reshape(tiles * TILE, CHUNK, D)
 
 
 def kernel(
-    x_ref, gain_attn, wq_ref, wp_ref, rel, gain_mlp, wu_ref, wd_ref,
+    x_ref, ga_ref, wq_ref, wp_ref, rb_ref, gm_ref, wu_ref, wd_ref,
     out_ref,
-    tokens, done, w_qkv, w_proj, w_up, w_down, qkv, mix, bias, strip, swap, ones,
+    tokens, done, gain_attn, gain_mlp, rel, w_qkv, w_proj, w_up, w_down, qkv, mix, bias, strip, swap, ones,
     weight_sem, in_sem, sent_sem, back_sem, out_sem,
 ):
     g1 = lax.axis_index("row")
     col = lax.axis_index("col")
-    g2, core = col // 2, col % 2
+    g2, core = lax.div(col, 2), lax.rem(col, 2)
     me = g1 * GRID + g2
-
-    def partner(t):
-        p1, p2 = lax.rem(g1 + t // GRID, GRID), lax.rem(g2 + lax.rem(t, GRID), GRID)
+    z_lo, x = lax.div(g1, 4), lax.rem(g1, 4)
+    y, z = lax.div(g2, 2), lax.rem(g2, 2) * 2 + z_lo
+    xs, ys, zs = ([lax.rem(v + k, 4) for k in range(4)] for v in (x, y, z))
+    z_highs = [lax.div(v, 2) for v in zs]
+    z_lows = [lax.rem(v, 2) for v in zs]
+
+    def partner(d):
+        p1 = z_lows[d[2]] * 4 + xs[d[0]]
+        p2 = ys[d[1]] * 2 + z_highs[d[2]]
         return p1 * GRID + p2, (p1, p2 * 2 + core)
 
     barrier = pltpu.get_barrier_semaphore()
-
-    @pl.loop(1, MEMBERS)
-    def _(t):
-        pl.semaphore_signal(barrier, inc=1, device_id=partner(t)[1], device_id_type=MESH)
-
-    weights = [
+    for d in ORDER:
+        pl.semaphore_signal(barrier, inc=1, device_id=partner(d)[1], device_id_type=MESH)
+
+    local = [
         pltpu.make_async_copy(src, dst, weight_sem.at[i])
-        for i, (src, dst) in enumerate(
-            ((wq_ref, w_qkv), (wp_ref, w_proj), (wu_ref, w_up), (wd_ref, w_down))
-        )
+        for i, (src, dst) in enumerate((
+            (rb_ref, rel), (ga_ref, gain_attn), (wq_ref, w_qkv), (wp_ref, w_proj),
+            (gm_ref, gain_mlp), (wu_ref, w_up), (wd_ref, w_down),
+        ))
     ]
+    for copy in local:
+        copy.start()
     for c in range(CHUNKS):
         pltpu.make_async_copy(
             x_ref.at[me, pl.ds(c * CHUNK, CHUNK)], tokens.at[c, me], in_sem.at[c]
         ).start()
-    for copy in weights:
-        copy.start()
     pl.semaphore_wait(barrier, MEMBERS - 1)
 
-    for c in range(CHUNKS):
-
-        @pl.loop(1, MEMBERS)
-        def _(t):
-            peer, device = partner(t)
+    def send(c):
+        for d in ORDER:
+            peer, device = partner(d)
             pltpu.make_async_remote_copy(
                 src_ref=x_ref.at[peer, pl.ds(c * CHUNK, CHUNK)],
                 dst_ref=tokens.at[c, me],
@@ -177,36 +194,11 @@
                 device_id_type=MESH,
             ).start()
 
-    fill_swap(swap)
-    fill_ones(ones)
-    fill_bias(rel, strip, bias)
-    for copy in weights:
-        copy.wait()
-
-    @pl.loop(0, CHUNKS)
-    def _(c):
-        here = tokens.at[c]
-        pltpu.make_async_copy(here, here, in_sem.at[c]).wait()
-
-        @pl.loop(0, MEMBERS // TILE // ATTN_TILES)
-        def _(step):
-            project(step, here, gain_attn[...][None], w_qkv, swap, qkv)
-
-        @pl.loop(0, CHUNK, unroll=True)
-        def _(b):
-            attend(b, qkv, bias, ones, mix)
-
-        @pl.loop(0, MEMBERS // TILE // MLP_TILES)
-        def _(step):
-            finish(
-                step, here, mix, swap, w_proj, gain_mlp[...][None], w_up, w_down, done.at[c]
-            )
-
-        @pl.loop(1, MEMBERS)
-        def _(t):
-            m, device = partner(t)
+    def send_back(c, order):
+        for d in order:
+            peer, device = partner(d)
             pltpu.make_async_remote_copy(
-                src_ref=done.at[c, m],
+                src_ref=done.at[c, peer],
                 dst_ref=out_ref.at[me, pl.ds(c * CHUNK, CHUNK)],
                 send_sem=back_sem.at[0],
                 recv_sem=out_sem.at[0],
@@ -214,9 +206,53 @@
                 device_id_type=MESH,
             ).start()
 
+    def keep(c):
         pltpu.make_async_copy(
             done.at[c, me], out_ref.at[me, pl.ds(c * CHUNK, CHUNK)], out_sem.at[0]
         ).start()
+
+    send(0)
+    send(1)
+    fill_swap(swap)
+    fill_ones(ones)
+    local[0].wait()
+    fill_bias(rel, strip, bias)
+    for copy in local[1:]:
+        copy.wait()
+
+    def attention(c):
+        here = tokens.at[c]
+        pltpu.make_async_copy(here, here, in_sem.at[c]).wait()
+        project(0, TILES, here, gain_attn[...][None], w_qkv, swap, qkv)
+        if not isinstance(c, int):
+
+            @pl.when(c < CHUNKS - 2)
+            def _():
+                send(c + 2)
+
+        @pl.loop(0, CHUNK, unroll=True)
+        def _(b):
+            attend(b, qkv, bias, ones, mix)
+
+    def rest(c, first, tiles):
+        finish(
+            first, tiles, tokens.at[c], mix, swap, w_proj, gain_mlp[...][None], w_up, w_down, done.at[c]
+        )
+
+    @pl.loop(0, CHUNKS - 1)
+    def _(c):
+        attention(c)
+        rest(c, 0, TILES)
+        send_back(c, ORDER)
+        keep(c)
+
+    last = CHUNKS - 1
+    attention(last)
+    rest(last, (1 - z_lo) * 2, 2)
+    send_back(last, [d for d in ORDER if d[2] % 2 == 1])
+    rest(last, z_lo * 2, 2)
+    send_back(last, [d for d in ORDER if d[2] % 2 == 0])
+    keep(last)
 
     pltpu.make_async_copy(out_ref, out_ref, out_sem.at[0]).wait()
     others = x_ref.at[pl.ds(0, MEMBERS - 1)]
@@ -224,18 +260,33 @@
     pltpu.make_async_copy(others, others, back_sem.at[0]).wait()
 
 
+def move(src, dst, sems):
+    parts = sems.shape[0]
+    step = src.shape[0] // parts
+    copies = [
+        pltpu.make_async_copy(src.at[pl.ds(i * step, step)], dst.at[pl.ds(i * step, step)], sems.at[i])
+        for i in range(parts)
+    ]
+    for copy in copies:
+        copy.start()
+    for copy in copies:
+        copy.wait()
+
+
 def on_device(tokens_map, gain_attn, w_qkv, w_proj, rel_bias, gain_mlp, w_up, w_down):
-    hbm = pl.BlockSpec(memory_space=pl.ANY)
-    vmem = pl.BlockSpec(memory_space=pltpu.VMEM)
-    return pl.pallas_call(
+    hbm = pl.BlockSpec(memory_space=pltpu.HBM)
+    arrived = pl.pallas_call(
         kernel,
         name="grid_block",
-        out_shape=jax.ShapeDtypeStruct(tokens_map.shape, bf16),
-        in_specs=[hbm, vmem, hbm, hbm, vmem, vmem, hbm, hbm],
-        out_specs=hbm,
+        out_shape=pltpu.VMEM(tokens_map.shape, bf16),
+        in_specs=[hbm] * 8,
+        out_specs=pl.BlockSpec(memory_space=pl.ANY),
         scratch_shapes=[
             pltpu.VMEM((CHUNKS, MEMBERS, CHUNK, D), bf16),
             pltpu.VMEM((CHUNKS, MEMBERS, CHUNK, D), bf16),
+            pltpu.VMEM((D,), f32),
+            pltpu.VMEM((D,), f32),
+            pltpu.VMEM((HEADS, 15, 15), f32),
             pltpu.VMEM((D, 3 * D), bf16),
             pltpu.VMEM((D, D), bf16),
             pltpu.VMEM((D, MLP_DIM), bf16),
@@ -246,16 +297,25 @@
             pltpu.VMEM((HEADS, GRID, 128), f32),
             pltpu.VMEM((256, 256), bf16),
             pltpu.VMEM((256, 128), bf16),
-            pltpu.SemaphoreType.DMA((4,)),
+            pltpu.SemaphoreType.DMA((7,)),
             pltpu.SemaphoreType.DMA((CHUNKS,)),
             pltpu.SemaphoreType.DMA((1,)),
             pltpu.SemaphoreType.DMA((1,)),
             pltpu.SemaphoreType.DMA((1,)),
         ],
         compiler_params=pltpu.CompilerParams(
-            collective_id=0, has_side_effects=True, vmem_limit_bytes=56 * 2**20
+            collective_id=0, has_side_effects=True, vmem_limit_bytes=44 * 2**20
         ),
-    )(tokens_map, gain_attn, w_qkv, w_proj, rel_bias, gain_mlp, w_up, w_down)
+    )(*(pltpu.with_memory_space_constraint(a, pltpu.HBM) for a in (tokens_map, gain_attn, w_qkv, w_proj, rel_bias, gain_mlp, w_up, w_down)))
+    return pl.pallas_call(
+        move,
+        name="move_out",
+        out_shape=jax.ShapeDtypeStruct(tokens_map.shape, bf16),
+        in_specs=[pl.BlockSpec(memory_space=pl.ANY)],
+        out_specs=hbm,
+        scratch_shapes=[pltpu.SemaphoreType.DMA((8,))],
+        compiler_params=pltpu.CompilerParams(vmem_limit_bytes=16 * 2**20),
+    )(arrived)
 
 
 def solution(mesh):

time: 85.3 us -> 81.6 us (0.957)
  local copies, waits for them, and re-layouts: 3.88 us -> 0 us
    unnamed x1 -> x0, local copies, waits for them, and re-layouts: 3.88 us -> none
    pallas_call x1 -> x2, Pallas kernels: 80.5 us -> 80.9 us  [the longest x1 79.2 us: on_device(): pl.pallas_call(kernel, name='grid_block', out_shape=pltpu.VMEM(tokens_map...]
where the time goes in v2:
time: 81.6 us; the launch traced here: 81.1 us
  Pallas kernels  80.9 us (99%)
    pallas_call x1, Pallas kernels, on_device(): pl.pallas_call(kernel, name='grid_block', out_shape=pltpu.VMEM(tokens_map...  79.2 us
    pallas_call x1, Pallas kernels, on_device(): pl.pallas_call(move, name='move_out', out_shape=jax.ShapeDtypeStruct(toke...  1.72 us

profile of v2, /device:TPU:1, one launch (start us, length us, event | category | flops | bytes accessed | tf_op | source)
XLA Modules:
  0.0 81.1 jit_solution(8228316753593935519)
XLA Ops:
  0.0 79.2 %grid_block.1.src = bf16[64,64,384]{2,1,0:T(8,128)(2,1)S(1)} custom-call(bf16[64,64,384]{2,1,0:T(8,128)(2,1)} %x_ref.1, f32[384]{0:T(512)} %ga_ref.1, bf16[384,1152]{1,0:T(8,128)(2,1)} %wq_ref.1, bf16[384,384]{1,0:T(8,128)(2,1)} %wp_ref.1, f32[12,15,15]{2,1,0:T(8,128)} %rb_ref.1, f32[384]{0:T(512)} %gm_ref.1, bf16[384,1536]{1,0:T(8,128)(2,1)} %wu_ref.1, ...), custom_call_target="tpu_custom_call" | custom-call | tf_op jit(solution)/shard_map/grid_block/pallas_call | solution.py:278
  79.2 1.7 %move_out.1 = bf16[64,64,384]{2,1,0:T(8,128)(2,1)} custom-call(bf16[64,64,384]{2,1,0:T(8,128)(2,1)S(1)} %grid_block.1.src), custom_call_target="tpu_custom_call" | custom-call | tf_op jit(solution)/shard_map/move_out/pallas_call | solution.py:310

commit v3 on v2

--- a/solution.py
+++ b/solution.py
@@ -40,6 +40,7 @@
 
 
 ORDER = displacements()
+LINES, PLANES, SPACE = ([d for d in ORDER if d.count(0) == 3 - n] for n in (1, 2, 3))
 
 
 def norm(values, gain):
@@ -146,7 +147,7 @@
     x_ref, ga_ref, wq_ref, wp_ref, rb_ref, gm_ref, wu_ref, wd_ref,
     out_ref,
     tokens, done, gain_attn, gain_mlp, rel, w_qkv, w_proj, w_up, w_down, qkv, mix, bias, strip, swap, ones,
-    weight_sem, in_sem, sent_sem, back_sem, out_sem,
+    heard, weight_sem, in_sem, sent_sem, back_sem, out_sem,
 ):
     g1 = lax.axis_index("row")
     col = lax.axis_index("col")
@@ -164,7 +165,7 @@
         return p1 * GRID + p2, (p1, p2 * 2 + core)
 
     barrier = pltpu.get_barrier_semaphore()
-    for d in ORDER:
+    for d in LINES:
         pl.semaphore_signal(barrier, inc=1, device_id=partner(d)[1], device_id_type=MESH)
 
     local = [
@@ -180,10 +181,9 @@
         pltpu.make_async_copy(
             x_ref.at[me, pl.ds(c * CHUNK, CHUNK)], tokens.at[c, me], in_sem.at[c]
         ).start()
-    pl.semaphore_wait(barrier, MEMBERS - 1)
-
-    def send(c):
-        for d in ORDER:
+
+    def send(c, order):
+        for d in order:
             peer, device = partner(d)
             pltpu.make_async_remote_copy(
                 src_ref=x_ref.at[peer, pl.ds(c * CHUNK, CHUNK)],
@@ -211,8 +211,22 @@
             done.at[c, me], out_ref.at[me, pl.ds(c * CHUNK, CHUNK)], out_sem.at[0]
         ).start()
 
-    send(0)
-    send(1)
+    def tell(round_):
+        for d in LINES:
+            pl.semaphore_signal(
+                heard.at[round_], inc=1, device_id=partner(d)[1], device_id_type=MESH
+            )
+
+    pl.semaphore_wait(barrier, len(LINES))
+    tell(0)
+    for c in range(CHUNKS):
+        send(c, LINES)
+    pl.semaphore_wait(heard.at[0], len(LINES))
+    tell(1)
+    send(0, PLANES)
+    pl.semaphore_wait(heard.at[1], len(LINES))
+    send(0, SPACE)
+    send(1, SPACE + PLANES)
     fill_swap(swap)
     fill_ones(ones)
     local[0].wait()
@@ -228,7 +242,7 @@
 
             @pl.when(c < CHUNKS - 2)
             def _():
-                send(c + 2)
+                send(c + 2, SPACE + PLANES)
 
         @pl.loop(0, CHUNK, unroll=True)
         def _(b):
@@ -297,6 +311,7 @@
             pltpu.VMEM((HEADS, GRID, 128), f32),
             pltpu.VMEM((256, 256), bf16),
             pltpu.VMEM((256, 128), bf16),
+            pltpu.SemaphoreType.REGULAR((2,)),
             pltpu.SemaphoreType.DMA((7,)),
             pltpu.SemaphoreType.DMA((CHUNKS,)),
             pltpu.SemaphoreType.DMA((1,)),

time: 81.6 us -> 80.6 us (0.988)
  no operation moved by 1% of the time
where the time goes in v3:
time: 80.6 us; the launch traced here: 80.5 us
  Pallas kernels  80.3 us (100%)
    pallas_call x1, Pallas kernels, on_device(): pl.pallas_call(kernel, name='grid_block', out_shape=pltpu.VMEM(tokens_map...  78.6 us
    pallas_call x1, Pallas kernels, on_device(): pl.pallas_call(move, name='move_out', out_shape=jax.ShapeDtypeStruct(toke...  1.72 us

profile of v3, /device:TPU:1, one launch (start us, length us, event | category | flops | bytes accessed | tf_op | source)
XLA Modules:
  0.0 80.5 jit_solution(1053651065528608919)
XLA Ops:
  0.0 78.6 %grid_block.1.src = bf16[64,64,384]{2,1,0:T(8,128)(2,1)S(1)} custom-call(bf16[64,64,384]{2,1,0:T(8,128)(2,1)} %x_ref.1, f32[384]{0:T(512)} %ga_ref.1, bf16[384,1152]{1,0:T(8,128)(2,1)} %wq_ref.1, bf16[384,384]{1,0:T(8,128)(2,1)} %wp_ref.1, f32[12,15,15]{2,1,0:T(8,128)} %rb_ref.1, f32[384]{0:T(512)} %gm_ref.1, bf16[384,1536]{1,0:T(8,128)(2,1)} %wu_ref.1, ...), custom_call_target="tpu_custom_call" | custom-call | tf_op jit(solution)/shard_map/grid_block/pallas_call | solution.py:292
  78.6 1.7 %move_out.1 = bf16[64,64,384]{2,1,0:T(8,128)(2,1)} custom-call(bf16[64,64,384]{2,1,0:T(8,128)(2,1)S(1)} %grid_block.1.src), custom_call_target="tpu_custom_call" | custom-call | tf_op jit(solution)/shard_map/move_out/pallas_call | solution.py:325

commit v4 on v3

--- a/solution.py
+++ b/solution.py
@@ -211,20 +211,22 @@
             done.at[c, me], out_ref.at[me, pl.ds(c * CHUNK, CHUNK)], out_sem.at[0]
         ).start()
 
-    def tell(round_):
-        for d in LINES:
+    def tell(round_, mates):
+        for d in mates:
             pl.semaphore_signal(
                 heard.at[round_], inc=1, device_id=partner(d)[1], device_id_type=MESH
             )
 
+    along_z = [d for d in LINES if d[2]]
+    across = [d for d in LINES if not d[2]]
     pl.semaphore_wait(barrier, len(LINES))
-    tell(0)
+    tell(0, across)
     for c in range(CHUNKS):
         send(c, LINES)
-    pl.semaphore_wait(heard.at[0], len(LINES))
-    tell(1)
+    pl.semaphore_wait(heard.at[0], len(across))
+    tell(1, along_z)
     send(0, PLANES)
-    pl.semaphore_wait(heard.at[1], len(LINES))
+    pl.semaphore_wait(heard.at[1], len(along_z))
     send(0, SPACE)
     send(1, SPACE + PLANES)
     fill_swap(swap)
@@ -328,7 +330,7 @@
         out_shape=jax.ShapeDtypeStruct(tokens_map.shape, bf16),
         in_specs=[pl.BlockSpec(memory_space=pl.ANY)],
         out_specs=hbm,
-        scratch_shapes=[pltpu.SemaphoreType.DMA((8,))],
+        scratch_shapes=[pltpu.SemaphoreType.DMA((2,))],
         compiler_params=pltpu.CompilerParams(vmem_limit_bytes=16 * 2**20),
     )(arrived)
 

time: 80.6 us -> 80.6 us (level)
  no operation moved by 1% of the time
where the time goes in v4:
time: 80.6 us; the launch traced here: 80.5 us
  Pallas kernels  80.4 us (100%)
    pallas_call x1, Pallas kernels, on_device(): pl.pallas_call(kernel, name='grid_block', out_shape=pltpu.VMEM(tokens_map...  78.7 us
    pallas_call x1, Pallas kernels, on_device(): pl.pallas_call(move, name='move_out', out_shape=jax.ShapeDtypeStruct(toke...  1.68 us

profile of v4, /device:TPU:1, one launch (start us, length us, event | category | flops | bytes accessed | tf_op | source)
XLA Modules:
  0.0 80.5 jit_solution(14286793657999528367)
XLA Ops:
  0.0 78.7 %grid_block.1.src = bf16[64,64,384]{2,1,0:T(8,128)(2,1)S(1)} custom-call(bf16[64,64,384]{2,1,0:T(8,128)(2,1)} %x_ref.1, f32[384]{0:T(512)} %ga_ref.1, bf16[384,1152]{1,0:T(8,128)(2,1)} %wq_ref.1, bf16[384,384]{1,0:T(8,128)(2,1)} %wp_ref.1, f32[12,15,15]{2,1,0:T(8,128)} %rb_ref.1, f32[384]{0:T(512)} %gm_ref.1, bf16[384,1536]{1,0:T(8,128)(2,1)} %wu_ref.1, ...), custom_call_target="tpu_custom_call" | custom-call | tf_op jit(solution)/shard_map/grid_block/pallas_call | solution.py:294
  78.7 1.7 %move_out.1 = bf16[64,64,384]{2,1,0:T(8,128)(2,1)} custom-call(bf16[64,64,384]{2,1,0:T(8,128)(2,1)S(1)} %grid_block.1.src), custom_call_target="tpu_custom_call" | custom-call | tf_op jit(solution)/shard_map/move_out/pallas_call | solution.py:327

commit v5 on v4

--- a/solution.py
+++ b/solution.py
@@ -40,6 +40,7 @@
 
 
 ORDER = displacements()
+MIXED = [d for pair in zip(ORDER, ORDER[::-1]) for d in pair][:len(ORDER)]
 LINES, PLANES, SPACE = ([d for d in ORDER if d.count(0) == 3 - n] for n in (1, 2, 3))
 
 
@@ -259,7 +260,7 @@
     def _(c):
         attention(c)
         rest(c, 0, TILES)
-        send_back(c, ORDER)
+        send_back(c, MIXED)
         keep(c)
 
     last = CHUNKS - 1

time: 80.6 us -> 80.6 us (level)
  no operation moved by 1% of the time
where the time goes in v5:
time: 80.6 us; the launch traced here: 80.5 us
  Pallas kernels  80.4 us (100%)
    pallas_call x1, Pallas kernels, on_device(): pl.pallas_call(kernel, name='grid_block', out_shape=pltpu.VMEM(tokens_map...  78.7 us
    pallas_call x1, Pallas kernels, on_device(): pl.pallas_call(move, name='move_out', out_shape=jax.ShapeDtypeStruct(toke...  1.68 us

profile of v5, /device:TPU:1, one launch (start us, length us, event | category | flops | bytes accessed | tf_op | source)
XLA Modules:
  0.0 80.5 jit_solution(6838082745216880326)
XLA Ops:
  0.0 78.7 %grid_block.1.src = bf16[64,64,384]{2,1,0:T(8,128)(2,1)S(1)} custom-call(bf16[64,64,384]{2,1,0:T(8,128)(2,1)} %x_ref.1, f32[384]{0:T(512)} %ga_ref.1, bf16[384,1152]{1,0:T(8,128)(2,1)} %wq_ref.1, bf16[384,384]{1,0:T(8,128)(2,1)} %wp_ref.1, f32[12,15,15]{2,1,0:T(8,128)} %rb_ref.1, f32[384]{0:T(512)} %gm_ref.1, bf16[384,1536]{1,0:T(8,128)(2,1)} %wu_ref.1, ...), custom_call_target="tpu_custom_call" | custom-call | tf_op jit(solution)/shard_map/grid_block/pallas_call | solution.py:295
  78.7 1.7 %move_out.1 = bf16[64,64,384]{2,1,0:T(8,128)(2,1)} custom-call(bf16[64,64,384]{2,1,0:T(8,128)(2,1)S(1)} %grid_block.1.src), custom_call_target="tpu_custom_call" | custom-call | tf_op jit(solution)/shard_map/move_out/pallas_call | solution.py:328
